TPU v7x, 32 devices: a whole 2x2x4 slice. The times are simulated.
32 devices in a mesh: dp: 4 (over y, x), ctx: 4 (over z), expert: 2 (over core).
Axes of the slice: x: 2, y: 2, z: 4, core: 2. Of those that a mesh axis runs over, the one named last changes fastest.
Arguments:
- inputs: bfloat16 [8, 2048, 768], P(('dp', 'expert'), 'ctx'), may hold values from -6 to 6
- cotangent: bfloat16 [8, 2048, 768], P(('dp', 'expert'), 'ctx'), may hold values from -6 to 6
- route: int32 [8, 2048, 1], P(('dp', 'expert'), 'ctx'), may hold values from 0 to 7
- arrival: int32 [8, 4, 512], P(('dp', 'expert'), 'ctx'), may hold values from 0 to 511, each once within a row
- branch: int32 [8, 4], P(('dp', 'expert'), 'ctx'), may hold values from 256 to 1024, as said below
- attn_gain: bfloat16 [768], replicated, may hold values from 0.5 to 1.5
- query_weight: bfloat16 [768, 768], replicated, may hold values from -0.0546875 to 0.0546875
- key_weight: bfloat16 [768, 768], replicated, may hold values from -0.21875 to 0.21875
- value_weight: bfloat16 [768, 768], replicated, may hold values from -0.21875 to 0.21875
- output_weight: bfloat16 [768, 768], replicated, may hold values from -0.875 to 0.875
- rel_table: bfloat16 [32, 12], replicated, may hold values from -3 to 3
- moe_gain: bfloat16 [768], replicated, may hold values from 0.5 to 1.5
- router_weight: bfloat16 [768, 8], replicated, may hold values from -0.15625 to 0.15625
- expert_in: bfloat16 [8, 768, 3072], P(('ctx', 'expert')), may hold values from -0.21875 to 0.21875
- expert_out: bfloat16 [8, 3072, 768], P(('ctx', 'expert')), may hold values from -0.875 to 0.875
Outputs:
- layer_out: bfloat16 [8, 2048, 768], P(('dp', 'expert'), 'ctx')
- input_grad: float32 [8, 2048, 768], P(('dp', 'expert'), 'ctx')
- attn_gain_grad: float32 [768], replicated
- query_weight_grad: float32 [768, 768], replicated
- key_weight_grad: float32 [768, 768], replicated
- value_weight_grad: float32 [768, 768], replicated
- output_weight_grad: float32 [768, 768], replicated
- table_grad: float32 [32, 12], replicated
- moe_gain_grad: float32 [768], replicated
- router_grad: float32 [768, 8], replicated
- expert_in_grad: float32 [8, 768, 3072], P(('ctx', 'expert'), None, 'dp')
- expert_out_grad: float32 [8, 3072, 768], P(('ctx', 'expert'), 'dp')
Inputs may be any that keep to these rules, and one draw needn't show every extreme that they name: `route`: every expert is named by some token. `arrival`: the 512 entries of one device block are a permutation; a smaller entry arrives earlier at its expert. Continuation c of group g follows the first branch[g, c] tokens of its prompt; in every group some continuation follows all 1024.
All inputs are finite; a program needn't handle non-finite values.
Results may differ from a plain program's by a relative error of at most 0.02.
Values may be sent and summed in bfloat16 or wider, within the bound.
A program may use at most 192 MiB of HBM per device.

v0:
```python
import functools

import jax
import jax.numpy as jnp
from jax import lax
from jax.experimental import pallas as pl
from jax.experimental.pallas import tpu as pltpu
from jax.sharding import PartitionSpec as P

PB = 256
TILE = 128
CHUNKS = 2

bucket_edges = (19, 21, 24, 27, 31, 35, 40, 46, 52, 59, 67, 77, 87, 99, 113)
norm_eps = 1e-06
masked_score = -1e30
gelu_scale = 0.7978845608
gelu_cube = 0.044715

bf16 = jnp.bfloat16
f32 = jnp.float32
VMEM_LIMIT = 121 * 512 * 1024


def dot_nn(a, b):
    return jnp.dot(a, b, preferred_element_type=f32)


def dot_nt(a, b):
    return lax.dot_general(a, b, (((1,), (1,)), ((), ())), preferred_element_type=f32)


def dot_tn(a, b):
    return lax.dot_general(a, b, (((0,), (0,)), ((), ())), preferred_element_type=f32)


def two_parts(a):
    high = a.astype(bf16)
    return high, (a - high.astype(f32)).astype(bf16)


def vmem():
    return pl.BlockSpec(memory_space=pltpu.VMEM)


def smem():
    return pl.BlockSpec(memory_space=pltpu.SMEM)


def params():
    return pltpu.CompilerParams(vmem_limit_bytes=VMEM_LIMIT)


def remote_params(number):
    return pltpu.CompilerParams(
        vmem_limit_bytes=VMEM_LIMIT, collective_id=number, has_side_effects=True
    )


def cost(flops, nbytes):
    return pl.CostEstimate(flops=int(flops), bytes_accessed=int(nbytes), transcendentals=0)


def shape(dims, kind):
    return jax.ShapeDtypeStruct(dims, kind)


def inverse_rms(x):
    return lax.rsqrt(jnp.mean(x * x, axis=-1, keepdims=True) + norm_eps)


def bucket_onehot(buckets):
    distance = jnp.arange(TILE, dtype=jnp.int32)
    ids = jnp.minimum(distance, 16)
    for edge in bucket_edges:
        ids = ids + (distance >= edge).astype(jnp.int32)
    return (ids[:, None] == jnp.arange(buckets, dtype=jnp.int32)[None, :]).astype(f32)


def near_index(first):
    rows = lax.broadcasted_iota(jnp.int32, (TILE, TILE), 0)
    lanes = lax.broadcasted_iota(jnp.int32, (TILE, TILE), 1)
    return first + lanes - rows


def near_tiles(ctx_at, plen):
    start = ctx_at * PB
    return (
        (start, 0, 0, False),
        (start, TILE, TILE, False),
        (start + TILE, TILE, 0, False),
        (plen, PB, 0, False),
        (plen, PB + TILE, TILE, False),
        (plen + TILE, PB + TILE, 0, False),
        (plen + PB, PB, TILE, False),
        (start - TILE, 0, TILE, True),
    )


def add_near(s_ref, bias_row, ctx_at, plen):
    source = jnp.broadcast_to(bias_row, (TILE, TILE))
    add_tiles(s_ref, source, ctx_at, near_tiles(ctx_at, plen))


def add_tiles(s_ref, source, ctx_at, tiles):
    for first_row, first_lane, gap, guarded in tiles:
        def work(first_row=first_row, first_lane=first_lane, gap=gap):
            rows = pl.ds(first_row if isinstance(first_row, int) else pl.multiple_of(first_row, 16), TILE)
            lanes = slice(first_lane, first_lane + TILE)
            index = jnp.clip(near_index(gap), 0, TILE - 1)
            s_ref[rows, lanes] = s_ref[rows, lanes] + jnp.take_along_axis(source, index, axis=1)

        if guarded:
            pl.when(ctx_at > 0)(work)
        else:
            work()


def scores_to(s_ref, keys, queries, plen):
    s_ref[:plen, :] = dot_nt(keys[:plen], queries)
    s_ref[plen:, PB:] = dot_nt(keys[plen:], queries[PB:])


def limits(ctx_at, branch, tokens):
    lane = lax.broadcasted_iota(jnp.int32, (1, tokens), 1)
    return jnp.where(lane < PB, ctx_at * PB + lane + 1, branch - TILE)


def window_rows(first, count, branch):
    rows = lax.broadcasted_iota(jnp.int32, (TILE, count), 0)
    places = lax.broadcasted_iota(jnp.int32, (TILE, count), 1) + first
    return (places == rows + (branch - TILE)).astype(bf16)


def row_steps(first, count, lanes):
    return first + lax.broadcasted_iota(jnp.int32, (count, lanes), 0)


def own_allowed(first, count, lanes):
    return row_steps(first, count, lanes) <= lax.broadcasted_iota(jnp.int32, (count, lanes), 1)


def head_lanes(half):
    return lax.broadcasted_iota(jnp.int32, (1, TILE), 1) // (TILE // 2) == half


def pick_rows(pieces, lanes):
    row = lax.broadcasted_iota(jnp.int32, (8, lanes), 0)
    return jnp.where(row == 0, pieces[0], jnp.where(row == 1, pieces[1], 0.0))


def fold8(x, op):
    return op(x.reshape(x.shape[0] // 8, 8, x.shape[1]), axis=0)


def owner_device(index):
    cores = lax.axis_size("expert")
    return {"ctx": index // cores, "expert": lax.rem(index, cores)}


def owners():
    cores = lax.axis_size("expert")
    count = cores * lax.axis_size("ctx")
    return count, lax.axis_index("ctx") * cores + lax.axis_index("expert")


def greet_owners():
    count, me = owners()
    barrier = pltpu.get_barrier_semaphore()

    def greet(ahead, _):
        pl.semaphore_signal(
            barrier, inc=1, device_id=owner_device(lax.rem(me + ahead, count)),
            device_id_type=pl.DeviceIdType.MESH,
        )
        return 0

    lax.fori_loop(1, count, greet, 0)
    pl.semaphore_wait(barrier, count - 1)


def block_copy(source, target, sems, ahead):
    count, me = owners()
    peer = lax.rem(me + ahead, count)
    return pltpu.make_async_remote_copy(
        src_ref=source.at[peer], dst_ref=target.at[me],
        send_sem=sems.at[0, ahead - 1], recv_sem=sems.at[1, ahead - 1],
        device_id=owner_device(peer), device_id_type=pl.DeviceIdType.MESH,
    )


def await_blocks(source, target, sems, sent, received):
    def one(ahead, _):
        copy = block_copy(source, target, sems, ahead)
        if received:
            copy.wait_recv()
        if sent:
            copy.wait_send()
        return 0

    lax.fori_loop(1, owners()[0], one, 0)


def place_rows(slot_row, index, block_rows, tokens):
    rows = lax.broadcasted_iota(jnp.int32, (block_rows, tokens), 0) + index * block_rows
    return (rows == slot_row).astype(bf16)


def front_kernel(
    capacity,
    branch_ref, bias_ref, x_ref, cot_ref, gain_ref, route_row, arrive_row,
    wq_ref, wk_ref, wv_ref,
    slot_out, cot_out, normed_own_out, normed_out, q_ref, k_out, v_out, att_out, lse_out,
    prompt_ref, send_ref, s_ref, p_ref, prompt_sems, cot_sems,
):
    branch = branch_ref[0, 0]
    ctx_at, ctx_count = lax.axis_index("ctx"), lax.axis_size("ctx")
    plen = PB * ctx_count
    tokens, width = x_ref.shape
    own = tokens - PB
    gain = gain_ref[...].astype(f32)
    count, me = owners()
    block_rows = send_ref.shape[1]
    greet_owners()

    chunk = PB // CHUNKS

    def pass_on(step, up, c):
        block = ctx_at - step if up else ctx_at + step
        ahead = ctx_at + 1 if up else ctx_at - 1
        fits = (block >= 0) & (ahead < ctx_count) if up else (block < ctx_count) & (ahead >= 0)
        piece = pl.ds(c * chunk, chunk)
        source = x_ref.at[piece] if step == 0 else prompt_ref.at[block, piece]
        copy = pltpu.make_async_remote_copy(
            src_ref=source, dst_ref=prompt_ref.at[block, piece],
            send_sem=prompt_sems.at[0, int(up), step, c], recv_sem=prompt_sems.at[1, int(up), step, c],
            device_id={"ctx": ahead}, device_id_type=pl.DeviceIdType.MESH,
        )
        return fits, copy

    def arrival(step, up, c):
        block = ctx_at - step - 1 if up else ctx_at + step + 1
        fits = block >= 0 if up else block < ctx_count
        place = prompt_ref.at[block, pl.ds(c * chunk, chunk)]
        copy = pltpu.make_async_remote_copy(
            src_ref=place, dst_ref=place,
            send_sem=prompt_sems.at[0, int(up), step, c], recv_sem=prompt_sems.at[1, int(up), step, c],
            device_id={"ctx": ctx_at}, device_id_type=pl.DeviceIdType.MESH,
        )
        return fits, block, copy

    for c in range(CHUNKS):
        for up in (True, False):
            fits, copy = pass_on(0, up, c)
            pl.when(fits)(copy.start)

    x = x_ref[...].astype(f32)
    normed_own_out[...] = (x * inverse_rms(x) * gain).astype(bf16)

    def column(i, _):
        cols = pl.ds(pl.multiple_of(i * 256, 256), 256)
        q_ref[:, cols] = dot_nn(normed_own_out[...], wq_ref[:, cols]).astype(bf16)
        k_out[plen : plen + own, cols] = dot_nn(normed_own_out[PB:, :], wk_ref[:, cols]).astype(bf16)
        v_out[plen : plen + own, cols] = dot_nn(normed_own_out[PB:, :], wv_ref[:, cols]).astype(bf16)
        return 0

    lax.fori_loop(0, width // 256, column, 0)

    def project(block):
        rows = pl.ds(pl.multiple_of(block * PB, PB), PB)

        def prompt_column(i, _):
            cols = pl.ds(pl.multiple_of(i * 256, 256), 256)
            k_out[rows, cols] = dot_nn(normed_out[rows, :], wk_ref[:, cols]).astype(bf16)
            v_out[rows, cols] = dot_nn(normed_out[rows, :], wv_ref[:, cols]).astype(bf16)
            return 0

        lax.fori_loop(0, width // 256, prompt_column, 0)

    def take(block):
        x = prompt_ref[block].astype(f32)
        rows = pl.ds(pl.multiple_of(block * PB, PB), PB)
        normed_out[rows, :] = (x * inverse_rms(x) * gain).astype(bf16)
        project(block)

    for step in range(ctx_count - 1):
        for c in range(CHUNKS):
            for up in (True, False):
                fits, block, copy = arrival(step, up, c)
                pl.when(fits)(copy.wait_recv)
                if step < ctx_count - 2:
                    fits, copy = pass_on(step + 1, up, c)
                    pl.when(fits)(copy.start)
        if step == 0:
            normed_out[pl.ds(pl.multiple_of(ctx_at * PB, PB), PB), :] = normed_own_out[:PB, :]
            project(ctx_at)
        for up in (True, False):
            fits, block, copy = arrival(step, up, 0)
            pl.when(fits)(functools.partial(take, block))

    def down(row):
        column = jnp.broadcast_to(row[...].astype(f32), (TILE, tokens)).T
        return jnp.concatenate([column] * (tokens // TILE), axis=1)

    same = down(route_row) == route_row[...].astype(f32)
    earlier = down(arrive_row) < arrive_row[...].astype(f32)
    rank = jnp.sum(jnp.where(same & earlier, 1.0, 0.0), axis=0, keepdims=True).astype(jnp.int32)
    slot = jnp.where(rank < capacity, route_row[...] * block_rows + rank, count * block_rows)
    slot_out[...] = slot

    def send_cot(ahead, _):
        peer = lax.rem(me + ahead, count)
        place = place_rows(slot_out[...], peer, block_rows, tokens)
        send_ref[peer] = dot_nn(place, cot_ref[...]).astype(bf16)
        block_copy(send_ref, cot_out, cot_sems, ahead).start()
        return 0

    def send_cots():
        lax.fori_loop(1, count, send_cot, 0)
        cot_out[me] = dot_nn(place_rows(slot_out[...], me, block_rows, tokens), cot_ref[...]).astype(bf16)

    def window_column(i, _):
        cols = pl.ds(pl.multiple_of(i * 256, 256), 256)
        window = window_rows(0, plen, branch)
        k_out[plen + own :, cols] = dot_nn(window, k_out[:plen, cols]).astype(bf16)
        v_out[plen + own :, cols] = dot_nn(window, v_out[:plen, cols]).astype(bf16)
        return 0

    lax.fori_loop(0, width // 256, window_column, 0)
    p_ref[plen:, :PB] = jnp.zeros((own + TILE, PB), bf16)
    limit = limits(ctx_at, branch, tokens)

    def pair(g, _):
        pl.when(g == 1)(send_cots)
        lanes = pl.ds(pl.multiple_of(g * TILE, TILE), TILE)
        queries = q_ref[:, lanes]
        keys = k_out[:, lanes]
        values_t = v_out[:, lanes].T
        bias = bias_ref[g]
        lse_rows, att_rows = [], []
        for half in range(2):
            scores_to(s_ref, jnp.where(head_lanes(half), keys, jnp.zeros_like(keys)), queries, plen)
            add_near(s_ref, bias[half : half + 1, :], ctx_at, plen)

            def top_of(i, top):
                for part in range(0, TILE, 32):
                    first = pl.multiple_of(i * TILE + part, 32)
                    rows = pl.ds(first, 32)
                    s = jnp.where(row_steps(first, 32, tokens) < limit, s_ref[rows, :], masked_score)
                    s_ref[rows, :] = s
                    top = jnp.maximum(top, fold8(s, jnp.max))
                return top

            top = lax.fori_loop(0, plen // TILE, top_of, jnp.full((8, tokens), masked_score, f32))
            own_top = jnp.full((8, own), masked_score, f32)
            for i in range(own // TILE + 1):
                rows = slice(plen + i * TILE, plen + (i + 1) * TILE)
                s = s_ref[rows, PB:]
                if i < own // TILE:
                    s = jnp.where(own_allowed(i * TILE, TILE, own), s, masked_score)
                    s_ref[rows, PB:] = s
                own_top = jnp.maximum(own_top, fold8(s, jnp.max))
            top = jnp.concatenate([top[:, :PB], jnp.maximum(top[:, PB:], own_top)], axis=1)
            top = jnp.max(top, axis=0, keepdims=True)

            def weigh(i, total):
                for part in range(0, TILE, 32):
                    rows = pl.ds(pl.multiple_of(i * TILE + part, 32), 32)
                    p = jnp.exp(s_ref[rows, :] - top)
                    p_ref[rows, :] = p.astype(bf16)
                    total = total + fold8(p, jnp.sum)
                return total

            total = lax.fori_loop(0, plen // TILE, weigh, jnp.zeros((8, tokens), f32))
            own_total = jnp.zeros((8, own), f32)
            for i in range(own // TILE + 1):
                rows = slice(plen + i * TILE, plen + (i + 1) * TILE)
                p = jnp.exp(s_ref[rows, PB:] - top[:, PB:])
                p_ref[rows, PB:] = p.astype(bf16)
                own_total = own_total + fold8(p, jnp.sum)
            total = jnp.concatenate([total[:, :PB], total[:, PB:] + own_total], axis=1)
            total = jnp.sum(total, axis=0, keepdims=True)
            rows = slice(half * 64, half * 64 + 64)
            att_rows.append((dot_nn(values_t[rows, :], p_ref[...]) / total).astype(bf16))
            lse_rows.append(top + jnp.log(total))
        att_out[lanes, :] = jnp.concatenate(att_rows, axis=0)
        lse_out[g] = pick_rows(lse_rows, tokens)
        return 0

    lax.fori_loop(0, width // TILE, pair, 0)
    await_blocks(send_ref, cot_out, cot_sems, True, True)
    for step in range(ctx_count - 1):
        for c in range(CHUNKS):
            for up in (True, False):
                fits, copy = pass_on(step, up, c)
                pl.when(fits)(copy.wait_send)


def router_probs(logits, lane, experts):
    logits = jnp.where(lane < experts, logits, masked_score)
    logits = jnp.exp(logits - jnp.max(logits, axis=1, keepdims=True))
    return logits / jnp.sum(logits, axis=1, keepdims=True)


def gelu_parts(v):
    t = jnp.tanh(gelu_scale * (v + gelu_cube * (v * v * v)))
    half = 0.5 * (1.0 + t)
    slope = half + 0.5 * v * (1.0 - t * t) * (gelu_scale + (3.0 * gelu_scale * gelu_cube) * (v * v))
    return v * half, slope


def expert_kernel(
    experts,
    att_ref, x_ref, wo_ref, gain_ref, router_ref, slot_row, cot_ref, cot_rows, win_hbm, wout_hbm,
    rows_out, router_out, hidden_grad_out, wo_grad_out, att_grad_out, delta_out, gain_grad_out,
    result_out, hidden_ref,
    moe_ref, send_ref, win_ref, wout_ref, group_rows, sent_ref, result_acc, grad_acc,
    grad_send, grad_recv, low_ref, att_t_ref, rows_sems, grad_sems, load_sems,
):
    tokens, width = x_ref.shape
    count, me = owners()
    block_rows = send_ref.shape[1]
    hidden_units = win_ref.shape[1]
    loads = [
        pltpu.make_async_copy(win_hbm, win_ref, load_sems.at[0]),
        pltpu.make_async_copy(wout_hbm, wout_ref, load_sems.at[1]),
    ]
    for copy in loads:
        copy.start()
    greet_owners()

    def column(i, _):
        cols = pl.ds(pl.multiple_of(i * 256, 256), 256)
        hidden_ref[:, cols] = x_ref[:, cols].astype(f32) + dot_tn(att_ref[...], wo_ref[:, cols])
        return 0

    lax.fori_loop(0, width // 256, column, 0)
    hidden = hidden_ref[...]
    moe_ref[...] = (hidden * inverse_rms(hidden) * gain_ref[...].astype(f32)).astype(bf16)

    members = 2 * lax.axis_size("expert") if lax.axis_size("ctx") % 2 == 0 else count
    groups = count // members
    my_group = me // members

    def send_rows(ahead, _):
        peer = lax.rem(me + ahead, count)
        place = place_rows(slot_row[...], peer, block_rows, tokens)
        send_ref[peer] = dot_nn(place, moe_ref[...]).astype(bf16)
        block_copy(send_ref, rows_out, rows_sems, ahead).start()
        return 0

    def send_group(g, _):
        base = lax.rem(my_group + g, groups) * members

        def member(i, _):
            ahead = lax.rem(base + i - me + count, count)
            pl.when(ahead > 0)(lambda: (send_rows(ahead, 0), None)[1])
            return 0

        return lax.fori_loop(0, members, member, 0)

    lax.fori_loop(0, groups, send_group, 0)
    rows_out[me] = dot_nn(place_rows(slot_row[...], me, block_rows, tokens), moe_ref[...]).astype(bf16)

    router_out[...] = jnp.zeros_like(router_out)
    for copy in loads:
        copy.wait()

    def group(g, _):
        base = lax.rem(my_group + g, groups) * members

        def arrive(i, _):
            behind = lax.rem(me - base - i + count, count)
            pl.when(behind > 0)(lambda: block_copy(send_ref, rows_out, rows_sems, behind).wait_recv())
            return 0

        lax.fori_loop(0, members, arrive, 0)
        blocks = pl.ds(base, members)
        size = members * block_rows
        group_rows[...] = rows_out[blocks].reshape(size, width)
        slot_lane = lax.broadcasted_iota(jnp.int32, (size, TILE), 1)
        mine = slot_lane == me
        probs = router_probs(dot_nn(group_rows[...], router_ref[...]), slot_lane, experts)
        gate = jnp.sum(jnp.where(mine, probs, 0.0), axis=1, keepdims=True)
        cot_group = cot_rows[blocks].reshape(size, width).astype(f32)
        sent_ref[...] = (gate * cot_group).astype(bf16)
        result_acc[...] = jnp.zeros_like(result_acc)
        grad_acc[...] = jnp.zeros_like(grad_acc)

        def units(i, _):
            cols = pl.ds(pl.multiple_of(i * width, width), width)
            act, slope = gelu_parts(dot_nn(group_rows[...], win_ref[:, cols]))
            result_acc[...] += dot_nn(act.astype(bf16), wout_ref[cols, :])
            pre_grad = (dot_nt(sent_ref[...], wout_ref[cols, :]) * slope).astype(bf16)
            grad_acc[...] += dot_nt(pre_grad, win_ref[:, cols])
            return 0

        lax.fori_loop(0, hidden_units // width, units, 0)
        result = result_acc[...].astype(bf16)
        gate_grad = jnp.sum(cot_group * result.astype(f32), axis=1, keepdims=True)
        logit_grad = (gate_grad * gate) * (jnp.where(mine, 1.0, 0.0) - probs)
        high, low = two_parts(logit_grad)
        grad = grad_acc[...] + (dot_nt(high, router_ref[...]) + dot_nt(low, router_ref[...]))
        grad_send[blocks] = grad.astype(bf16).reshape(members, block_rows, width)
        gated = (gate * result.astype(f32)).astype(bf16)
        result_out[blocks] = gated.reshape(members, block_rows, width)

        def give(i, _):
            ahead = lax.rem(base + i - me + count, count)

            @pl.when(ahead > 0)
            def _():
                block_copy(grad_send, grad_recv, grad_sems, ahead).start()

            return 0

        lax.fori_loop(0, members, give, 0)
        router_out[...] += dot_tn(high, group_rows[...]) + dot_tn(low, group_rows[...])
        return 0

    lax.fori_loop(0, groups, group, 0)
    grad_recv[me] = grad_send[me]

    slots = count * block_rows
    place = place_rows(slot_row[...], 0, slots, tokens)
    await_blocks(grad_send, grad_recv, grad_sems, False, True)
    moe_grad = dot_tn(place, grad_recv[...].reshape(slots, width))
    hidden = hidden_ref[...]
    inverse = inverse_rms(hidden)
    scaled = hidden * inverse
    gain_grad_out[...] = jnp.sum(moe_grad * scaled, axis=0, keepdims=True)
    through = moe_grad * gain_ref[...].astype(f32)
    shared = jnp.mean(through * scaled, axis=1, keepdims=True)
    hidden_grad = cot_ref[...].astype(f32) + inverse * (through - scaled * shared)
    hidden_grad_out[...] = hidden_grad
    low_ref[...] = hidden_grad.astype(bf16)

    def back_column(i, _):
        cols = pl.ds(pl.multiple_of(i * 256, 256), 256)
        wo_grad = dot_nn(att_ref[...], low_ref[:, cols]).astype(bf16)
        wo_grad_out[:, :, cols] = wo_grad.reshape(width // 16, 16, 256)
        att_grad_out[:, cols] = dot_nt(low_ref[...], wo_ref[cols, :]).astype(bf16)
        att_t_ref[cols, :] = dot_nt(wo_ref[cols, :], low_ref[...]).astype(bf16)
        return 0

    lax.fori_loop(0, width // 256, back_column, 0)

    def pair(g, _):
        rows = pl.ds(pl.multiple_of(g * TILE, TILE), TILE)
        both = att_ref[rows, :].astype(f32) * att_t_ref[rows, :].astype(f32)
        delta_out[g] = pick_rows(
            [jnp.sum(both[:64], axis=0, keepdims=True), jnp.sum(both[64:], axis=0, keepdims=True)],
            tokens,
        )
        return 0

    lax.fori_loop(0, width // TILE, pair, 0)
    await_blocks(send_ref, rows_out, rows_sems, True, False)
    await_blocks(grad_send, grad_recv, grad_sems, True, False)


class Axis:
    def __init__(self, name, size, step=1):
        place = lax.axis_index(name)
        self.name, self.size, self.step, self.place = name, size, step, place
        self.index = lax.rem(place // step, size)

    def at(self, ahead):
        return lax.rem(self.index + ahead, self.size)

    def peer(self, ahead):
        return {self.name: self.place + (self.at(ahead) - self.index) * self.step}


def mesh_axes():
    dp, ctx, expert = lax.axis_size("dp"), lax.axis_size("ctx"), lax.axis_size("expert")
    cores, lines = Axis("expert", expert), Axis("ctx", ctx)
    if dp == 4:
        near, far = Axis("dp", 2, 1), Axis("dp", 2, 2)
        return [[cores, near, far, lines], [cores, far, near, lines]]
    return [[cores, Axis("dp", dp), lines]] * 2


def push(source, target, sems, slot, device):
    copy = pltpu.make_async_remote_copy(
        src_ref=source, dst_ref=target, send_sem=sems.at[0, slot], recv_sem=sems.at[1, slot],
        device_id=device, device_id_type=pl.DeviceIdType.MESH,
    )
    copy.start()
    return copy


def back_kernel(
    experts, plan,
    branch_ref, bias_ref, q_ref, k_hbm, v_hbm, att_grad_ref, lse_ref, delta_ref, normed_hbm, normed_own_ref,
    gain_ref, wq_ref, wk_ref, wv_ref, wo_part_hbm, moe_gain_ref, router_part_hbm, x_hbm, hidden_grad_hbm,
    hidden_hbm, slot_row, result_hbm, rows_hbm, cot_hbm, win_hbm, wout_hbm, router_ref,
    full_ref, small_out, input_out, in_out, out_out, layer_out, rows_all,
    k_ref, v_ref, normed_ref, s_ref, dp_ref, p_ref, ds_ref, dq_ref, dk_ref, dv_ref, window_k, window_v, picked_ref,
    hist_ref, gain_sum,
    local_ref, shared_send, shared_recv, parts_ref, acc_refs, recv_refs, small_ref, small_recv,
    result_recv, win_ref, wout_ref, rows_ref, cot_ref, rows_t,
    block_sems, load_sems, sems, small_sems, shared_sems, result_sems, rows_sems,
):
    group, pieces, lengths = plan
    flows = mesh_axes()
    branch = branch_ref[0, 0]
    ctx_at = lax.axis_index("ctx")
    ctx_count, dp_count = lax.axis_size("ctx"), lax.axis_size("dp")
    tokens, width = q_ref.shape
    own = tokens - PB
    plen = PB * ctx_count
    count, me = owners()
    lines, columns_dp = Axis("ctx", ctx_count), Axis("dp", dp_count)
    whole_axes = [Axis("expert", lax.axis_size("expert")), columns_dp, lines]
    gain = gain_ref[...].astype(f32)
    limit = limits(ctx_at, branch, tokens)
    blocks = ctx_count + 2
    rows_16 = width // 16

    def block_loads(i):
        size = TILE if i == 1 else PB
        rows = (plen, plen + own)[i] if i < 2 else pl.multiple_of(lines.at(i - 1) * PB, PB)
        sources = [(k_hbm, k_ref, 0), (v_hbm, v_ref, 1)]
        if 2 <= i < blocks - 1:
            sources.append((normed_hbm, normed_ref, 2))
        return [
            pltpu.make_async_copy(
                source.at[pl.ds(rows, size)], target.at[i % 2, pl.ds(0, size)], block_sems.at[i, n]
            )
            for source, target, n in sources
        ]

    for copy in block_loads(0):
        copy.start()
    slice_width = win_ref.shape[1]
    part = pl.ds(pl.multiple_of(lax.axis_index("dp") * slice_width, slice_width), slice_width)
    weight_loads = [
        pltpu.make_async_copy(win_hbm.at[:, part], win_ref, load_sems.at[0]),
        pltpu.make_async_copy(wout_hbm.at[part], wout_ref, load_sems.at[1]),
    ]
    own_result = pltpu.make_async_copy(result_hbm.at[me], result_recv.at[me], load_sems.at[2])
    wo_load = pltpu.make_async_copy(wo_part_hbm, parts_ref.at[pl.ds(0, rows_16)], load_sems.at[5 + 2 * dp_count])
    router_load = pltpu.make_async_copy(
        router_part_hbm.at[pl.ds(0, experts)], small_ref.at[pl.ds(0, experts)], load_sems.at[7 + 2 * dp_count]
    )
    for copy in [wo_load, *weight_loads, own_result, router_load]:
        copy.start()

    barrier = pltpu.get_barrier_semaphore()

    def greet(ahead, _):
        pl.semaphore_signal(
            barrier, inc=1, device_id=owner_device(lax.rem(me + ahead, count)),
            device_id_type=pl.DeviceIdType.MESH,
        )
        return 0

    lax.fori_loop(1, count, greet, 0)
    for ahead in range(1, dp_count):
        pl.semaphore_signal(
            barrier, inc=1, device_id=columns_dp.peer(ahead), device_id_type=pl.DeviceIdType.MESH
        )
    pl.semaphore_wait(barrier, count - 1 + dp_count - 1)

    slots_of = {}

    def slot(*key):
        return slots_of.setdefault(key, len(slots_of))

    started = []

    def reduce_start(j, s):
        axis, length = flows[j % 2][s], lengths[s]
        copies = []
        for ahead in range(1, axis.size):
            target = axis.at(ahead)
            if s == 0:
                source = parts_ref.at[pl.ds(j * group + target * length, length)]
            else:
                source = acc_refs[s - 1].at[j, pl.ds(target * length, length)]
            there = recv_refs[s].at[j, ahead - 1]
            copies.append(push(source, there, sems, slot("r", j, s, ahead), axis.peer(ahead)))
        started.extend(copies)
        return copies

    def base_of(j, s):
        base = j * group
        for t in range(s + 1):
            base = base + flows[j % 2][t].index * lengths[t]
        return base

    def reduce_finish(j, s, copies):
        axis, length = flows[j % 2][s], lengths[s]
        for copy in copies:
            copy.wait_recv()
        last = s == len(lengths) - 1

        size = 4 if length % 4 == 0 else 1

        def some(u, _):
            if s == 0:
                total = parts_ref[pl.ds(base_of(j, 0) + u * size, size)].astype(f32)
            else:
                total = acc_refs[s - 1][j, pl.ds(axis.index * length + u * size, size)].astype(f32)
            for ahead in range(1, axis.size):
                total = total + recv_refs[s][j, ahead - 1, pl.ds(u * size, size)].astype(f32)
            if last:
                full_ref[pl.ds(base_of(j, s) + u * size, size)] = total.astype(bf16)
            else:
                acc_refs[s][j, pl.ds(u * size, size)] = total.astype(bf16)
            return 0

        lax.fori_loop(0, length // size, some, 0)

    def spread_start(j, s):
        axis, length = flows[j % 2][s], lengths[s]
        here = full_ref.at[pl.ds(base_of(j, s), length)]
        copies = [
            push(here, here, sems, slot("s", j, s, ahead), axis.peer(ahead))
            for ahead in range(1, axis.size)
        ]
        started.extend(copies)
        return copies

    def small_slot(s, ahead):
        return sum(axis.size - 1 for axis in whole_axes[:s]) + ahead - 1

    def small_start(s):
        axis = whole_axes[s]
        copies = [
            push(small_ref, small_recv[s].at[ahead - 1], small_sems, small_slot(s, ahead), axis.peer(ahead))
            for ahead in range(1, axis.size)
        ]
        return copies

    def small_finish(s, copies):
        axis = whole_axes[s]
        for copy in copies:
            copy.wait()
        mine = small_ref[...]
        total = jnp.zeros_like(mine)
        for index in range(axis.size):
            piece = mine
            for ahead in range(1, axis.size):
                piece = jnp.where(axis.at(axis.size - ahead) == index, small_recv[s][ahead - 1], piece)
            total = total + piece
        if s == len(whole_axes) - 1:
            small_out[...] = total
        else:
            small_ref[...] = total

    stages = len(lengths)
    early = pieces > 1 and group <= rows_16
    begin = [blocks + j // 2 for j in range(pieces)]
    if early:
        begin = [blocks - 1] + [blocks + (j - 1) // 2 for j in range(1, pieces)]
    pending = {}

    def advance(time):
        for j in sorted(range(pieces), key=lambda j: begin[j]):
            s = time - begin[j]
            if not 0 <= s < 2 * stages:
                continue
            if s < stages:
                reduce_finish(j, s, pending[j, s])
                if s + 1 < stages:
                    pending[j, s + 1] = reduce_start(j, s + 1)
                else:
                    pending[j, s + 1] = spread_start(j, s)
            else:
                for copy in pending[j, s]:
                    copy.wait_recv()
                if s + 1 < 2 * stages:
                    pending[j, s + 1] = spread_start(j, 2 * stages - 1 - (s + 1))

    def put(first, cols, value):
        rows = value.shape[0]
        parts_ref[first // 16 : (first + rows) // 16, :, cols] = value.astype(bf16).reshape(
            rows // 16, 16, value.shape[1]
        )

    def columns(work):
        def column(i, _):
            work(pl.ds(pl.multiple_of(i * 256, 256), 256))
            return 0

        lax.fori_loop(0, width // 256, column, 0)

    if parts_ref.shape[0] > 4 * rows_16:
        extra = parts_ref.shape[0] - 4 * rows_16
        parts_ref[4 * rows_16 :] = jnp.zeros((extra, 16, width), bf16)
    wo_load.wait()
    if early:
        pending[0, 0] = reduce_start(0, 0)

    def give_result(ahead, _):
        block_copy(result_hbm, result_recv, result_sems, ahead).start()
        return 0

    lax.fori_loop(1, count, give_result, 0)

    def rows_copy(ahead, e):
        return pltpu.make_async_remote_copy(
            src_ref=rows_hbm.at[e], dst_ref=rows_all.at[ahead - 1, e],
            send_sem=rows_sems.at[0, ahead - 1, e], recv_sem=rows_sems.at[1, ahead - 1, e],
            device_id=columns_dp.peer(ahead), device_id_type=pl.DeviceIdType.MESH,
        )

    def each_row_block(act):
        def one(e, _):
            for ahead in range(1, dp_count):
                act(rows_copy(ahead, e))
            return 0

        lax.fori_loop(0, count, one, 0)

    each_row_block(lambda copy: copy.start())

    shared_copies = []
    shared_slots = shared_send.shape[0]
    hist_ref[...] = jnp.zeros_like(hist_ref)
    gain_sum[...] = jnp.zeros_like(gain_sum)
    for i in range(blocks):
        cont, window, at_home = i == 0, i == 1, i == blocks - 1
        remote = i - 1
        size = TILE if window else PB
        for copy in block_loads(i):
            copy.wait()
        if i + 1 < blocks:
            for copy in block_loads(i + 1):
                copy.start()
        block = lines.at(max(remote, 0))
        lanes_from = PB if cont or window else 0
        lanes_used = slice(lanes_from, tokens)
        if cont or at_home:
            near = [
                (0, lanes_from, 0, None),
                (0, lanes_from + TILE, TILE, None),
                (TILE, lanes_from + TILE, 0, None),
            ]
        elif window:
            near = [(0, PB, TILE, None)]
        else:
            near = [(TILE, 0, TILE, block == ctx_at - 1)]

        if not (cont or window):
            places = lax.broadcasted_iota(jnp.int32, (PB, TILE), 0) + block * PB
            picks = lax.broadcasted_iota(jnp.int32, (PB, TILE), 1) + (branch - TILE)
            picked_ref[...] = (places == picks).astype(bf16)

        def pair(g, _, i=i, cont=cont, window=window, size=size, block=block, lanes_used=lanes_used, near=near):
            lanes = pl.ds(pl.multiple_of(g * TILE, TILE), TILE)
            queries = q_ref[lanes_used, lanes]
            grads = att_grad_ref[lanes_used, lanes]
            keys = k_ref[i % 2, :size, lanes]
            values = v_ref[i % 2, :size, lanes]
            keys_t = keys.T
            bias = bias_ref[g]
            dk_parts, dv_parts, dq_parts = [], [], []
            stacked = s_ref.shape[0] // PB
            for halves in [(0, 1)] if stacked == 2 else [(0,), (1,)]:
                total = len(halves) * size

                def masked(rows):
                    return jnp.concatenate([jnp.where(head_lanes(h), rows, jnp.zeros_like(rows)) for h in halves])

                s_ref[:total, lanes_used] = dot_nt(masked(keys), queries)
                dp_ref[:total, lanes_used] = dot_nt(masked(values), grads)
                for n, half in enumerate(halves):
                    offset = n * size
                    lse = lse_ref[g][half : half + 1, lanes_used]
                    delta = delta_ref[g][half : half + 1, lanes_used]
                    source = jnp.broadcast_to(bias[half : half + 1, :], (TILE, TILE))
                    for first, lane, gap, when in near:
                        def add(first=first + offset, lane=lane, gap=gap):
                            there = (slice(first, first + TILE), slice(lane, lane + TILE))
                            index = jnp.clip(near_index(gap), 0, TILE - 1)
                            s_ref[there] = s_ref[there] + jnp.take_along_axis(source, index, axis=1)

                        add() if when is None else pl.when(when)(add)
                    step = 32
                    for first in range(0, size, step):
                        rows = slice(offset + first, offset + first + step)
                        p = jnp.exp(s_ref[rows, lanes_used] - lse)
                        if cont:
                            p = jnp.where(own_allowed(first, step, own), p, 0.0)
                        elif not window:
                            p = jnp.where(row_steps(block * PB + first, step, tokens) < limit, p, 0.0)
                        p_ref[rows, lanes_used] = p.astype(bf16)
                        ds_ref[rows, lanes_used] = (p * (dp_ref[rows, lanes_used] - delta)).astype(bf16)
                    for first, lane, gap, when in near:
                        def collect(first=first + offset, lane=lane, gap=gap, half=half):
                            tile = ds_ref[first : first + TILE, lane : lane + TILE].astype(f32)
                            if gap > 0:
                                tile = jnp.where(near_index(gap) < TILE, tile, 0.0)
                            turn = lax.broadcasted_iota(jnp.int32, (TILE, TILE), 1) + lax.broadcasted_iota(
                                jnp.int32, (TILE, TILE), 0
                            )
                            tile = jnp.take_along_axis(tile, (turn - gap) & (TILE - 1), axis=1)
                            hist_ref[g * 2 + half] += fold8(tile, jnp.sum)

                        collect() if when is None else pl.when(when)(collect)
                dv_all = dot_nn(p_ref[:total, lanes_used], grads)
                dk_all = dot_nn(ds_ref[:total, lanes_used], queries)
                for n, half in enumerate(halves):
                    rows = slice(n * size, n * size + size)
                    dv_parts.append(dv_all[rows])
                    dk_parts.append(dk_all[rows])
                    dq_parts.append(dot_nn(keys_t[half * 64 : half * 64 + 64, :], ds_ref[rows, lanes_used]))
            dq = jnp.concatenate(dq_parts, axis=0)
            if cont:
                dq_ref[lanes, :PB] = jnp.zeros((TILE, PB), f32)
                dq_ref[lanes, PB:] = dq
            else:
                dq_ref[lanes, lanes_used] += dq
            mine = head_lanes(0)
            dv, dk = jnp.where(mine, dv_parts[0], dv_parts[1]), jnp.where(mine, dk_parts[0], dk_parts[1])
            if window:
                window_v[:, lanes], window_k[:, lanes] = dv.astype(bf16), dk.astype(bf16)
            else:
                if not cont:
                    dv = dv + dot_nn(picked_ref[...], window_v[:, lanes])
                    dk = dk + dot_nn(picked_ref[...], window_k[:, lanes])
                dv_ref[:, lanes], dk_ref[:, lanes] = dv.astype(bf16), dk.astype(bf16)
            return 0

        lax.fori_loop(0, width // TILE, pair, 0)

        def block_column(cols, i=i, cont=cont, at_home=at_home, remote=remote):
            if cont:
                normed = normed_own_ref[PB:, cols]
            elif at_home:
                normed = normed_own_ref[:PB, cols]
            else:
                normed = normed_ref[i % 2, :, cols]
            wk_part = dot_nn(rows_t[:, :PB], dk_ref[:, cols])
            wv_part = dot_nn(rows_t[:, :PB], dv_ref[:, cols])
            if cont:
                in_out[:, cols] = wk_part
                out_out[:, cols] = wv_part
            elif not at_home:
                in_out[:, cols] += wk_part
                out_out[:, cols] += wv_part
            else:
                put(width, cols, out_out[:, cols] + wv_part)
                put(2 * width, cols, in_out[:, cols] + wk_part)
            grad = dot_nt(dk_ref[...], wk_ref[cols, :]) + dot_nt(dv_ref[...], wv_ref[cols, :])
            gain_sum[:, cols] += jnp.sum(grad * normed.astype(f32), axis=0, keepdims=True)
            if cont:
                local_ref[PB:, cols] = grad
            elif at_home:
                local_ref[:PB, cols] = grad
            else:
                shared_send[(remote - 1) % shared_slots, :, cols] = grad.astype(bf16)

        if window:
            continue
        if shared_slots < remote < ctx_count:
            shared_copies[remote - 1 - shared_slots].wait_send()
        if cont:
            rows_t[:, :PB] = normed_own_ref[PB:, :].T
        elif at_home:
            rows_t[:, :PB] = normed_own_ref[:PB, :].T
        else:
            rows_t[:, :PB] = normed_ref[i % 2].T
        columns(block_column)
        if 1 <= remote < ctx_count:
            n = remote - 1
            shared_copies.append(
                push(shared_send.at[n % shared_slots], shared_recv.at[n], shared_sems, n, lines.peer(remote))
            )
    started.extend(shared_copies[-shared_slots:])

    def ready(j):
        if j > 0 or not early:
            pending[j, 0] = reduce_start(j, 0)

    done = 3 * rows_16
    for j in range(pieces):
        if (j + 1) * group <= done:
            ready(j)
    rows_ref[:tokens, :] = dq_ref[...].T.astype(bf16)
    rows_t[:, :tokens] = normed_own_ref[...].T

    def query_column(cols):
        put(3 * width, cols, dot_nn(rows_t[:, :tokens], rows_ref[:tokens, cols]))

    columns(query_column)
    for j in range(pieces):
        if (j + 1) * group > done:
            ready(j)

    def query_grad(cols):
        grad = dot_nt(rows_ref[:tokens, :], wq_ref[cols, :])
        gain_sum[:, cols] += jnp.sum(grad * normed_own_ref[:, cols].astype(f32), axis=0, keepdims=True)
        local_ref[:, cols] += grad

    columns(query_grad)
    small_ref[experts:, :] = jnp.zeros((small_ref.shape[0] - experts, width), f32)
    small_ref[experts : experts + 1, :] = gain_sum[...] / gain
    small_ref[experts + 1 : experts + 2, :] = moe_gain_ref[...]
    router_load.wait()
    per_row = width // TILE
    for head in range(hist_ref.shape[0]):
        row, lane = 2 + experts + head // per_row, head % per_row * TILE
        small_ref[row : row + 1, lane : lane + TILE] = jnp.sum(hist_ref[head], axis=0, keepdims=True)
    small_pending = small_start(0)

    slots = rows_ref.shape[0]

    def rows_load(n):
        source = rows_hbm if n == 0 else rows_all.at[n - 1]
        return pltpu.make_async_copy(source, result_recv, load_sems.at[3 + 2 * n])

    hidden_load = pltpu.make_async_copy(hidden_hbm, input_out, load_sems.at[4 + 2 * dp_count])
    hidden_load.start()
    grad_load = pltpu.make_async_copy(hidden_grad_hbm, input_out, load_sems.at[3 + 2 * dp_count])
    x_loads = [
        pltpu.make_async_copy(x_hbm.at[pl.ds(n * PB, PB)], normed_ref.at[n], load_sems.at[6 + 2 * dp_count + 2 * n])
        for n in range(2)
    ]
    for copy in x_loads:
        copy.start()

    def grads_of(n, c):
        if c == 0:
            if n == 0:
                for copy in weight_loads:
                    copy.wait()
            rows_load(n).wait()
            rows_ref[...] = result_recv[...].reshape(slots, width)
            cot_from = columns_dp.at(dp_count - n)
            load = pltpu.make_async_copy(cot_hbm.at[cot_from], result_recv, load_sems.at[4 + 2 * n])
            load.start()
            lane = lax.broadcasted_iota(jnp.int32, (slots, TILE), 1)
            probs = router_probs(dot_nn(rows_ref[...], router_ref[...]), lane, experts)
            gate = jnp.sum(jnp.where(lane == me, probs, 0.0), axis=1, keepdims=True)
            load.wait()
            cot = result_recv[...].reshape(slots, width)
            cot_ref[...] = (gate * cot.astype(f32)).astype(bf16)
            if n == 0:
                each_row_block(lambda copy: copy.wait_recv())
            if n + 1 < dp_count:
                rows_load(n + 1).start()
            rows_t[...] = rows_ref[...].T
        cols = slice(c * 256, c * 256 + 256)
        act, slope = gelu_parts(dot_nn(rows_ref[...], win_ref[:, cols]))
        pre_grad = (dot_nt(cot_ref[...], wout_ref[cols, :]) * slope).astype(bf16)
        out_part = dot_tn(act.astype(bf16), cot_ref[...])
        in_part = dot_nn(rows_t[...], pre_grad)
        if n == 0:
            out_out[cols, :] = out_part
            in_out[:, cols] = in_part
        else:
            out_out[cols, :] += out_part
            in_out[:, cols] += in_part

    def input_back():
        for copy in shared_copies:
            copy.wait_recv()
        for copy in x_loads:
            copy.wait()
        grad_load.wait()
        for first, shared_rows in ((0, True), (PB, False)):
            rows = slice(first, PB if shared_rows else tokens)
            x = normed_ref[0 if shared_rows else 1].astype(f32)
            inverse = inverse_rms(x)
            grad = local_ref[rows, :]
            if shared_rows:
                for n in range(ctx_count - 1):
                    grad = grad + shared_recv[n].astype(f32)
            through = grad * gain
            scaled = x * inverse
            shared = jnp.mean(through * scaled, axis=1, keepdims=True)
            input_out[rows, :] += inverse * (through - scaled * shared)

    def layer():
        own_result.wait()
        await_blocks(result_hbm, result_recv, result_sems, False, True)
        place = place_rows(slot_row[...], 0, slots, tokens)
        returned = dot_tn(place, result_recv[...].reshape(slots, width))
        hidden_load.wait()
        layer_out[...] = (input_out[...] + returned).astype(bf16)
        rows_load(0).start()
        grad_load.start()

    work = [layer]
    work += [functools.partial(grads_of, n, c) for n in range(dp_count) for c in range(slice_width // 256)]
    work += [input_back]
    for time in range(blocks - 1, max(begin) + 2 * stages):
        if time >= blocks:
            advance(time)
        elif early:
            advance(time)
        s = time - blocks
        if 0 <= s < len(whole_axes):
            small_finish(s, small_pending)
            if s + 1 < len(whole_axes):
                small_pending = small_start(s + 1)
        for _ in range(-(-len(work) // (max(begin) + 2 * stages - time))):
            work.pop(0)()
    for copy in started:
        copy.wait_send()
    await_blocks(result_hbm, result_recv, result_sems, True, False)
    each_row_block(lambda copy: copy.wait_send())


def finish_kernel(full_ref, in_ref, out_ref, input_ref, layer_ref, *results):
    weights, rest = results[:4], results[4:]
    for n, weight in enumerate(weights):
        weight[...] = full_ref[n].astype(f32).reshape(weight.shape)
    for source, target in zip((in_ref, out_ref, input_ref, layer_ref), rest):
        target[...] = source[...]


def tail_plan(sizes, width):
    group = 1
    for size in sizes:
        group *= size
    units = 4 * width // 16
    pieces = -(-units // group)
    lengths, left = [], group
    for size in sizes:
        left //= size
        lengths.append(left)
    return group, pieces, lengths


def body(
    inputs, cotangent, route, arrival, branch, attn_gain, query_weight, key_weight, value_weight,
    output_weight, rel_table, moe_gain, router_weight, expert_in, expert_out,
):
    x = inputs[0]
    cot = cotangent[0]
    tokens, width = x.shape
    own = tokens - PB
    buckets, heads = rel_table.shape
    experts = router_weight.shape[1]
    capacity = 9 * tokens // (8 * experts)
    block_rows = capacity if capacity % 8 == 0 else -(-capacity // 16) * 16
    slots = experts * block_rows
    ctx_count = lax.axis_size("ctx")
    dp_count = lax.axis_size("dp")
    plen = PB * ctx_count
    keys_total = plen + own + TILE
    hidden_units = expert_in.shape[2]
    pairs = width // TILE
    attn_gain_row = attn_gain.reshape(1, width)
    moe_gain_row = moe_gain.reshape(1, width)
    onehot = bucket_onehot(buckets)
    by_distance = jnp.dot(onehot, rel_table.astype(f32), precision=lax.Precision.HIGHEST).T
    by_distance = by_distance - by_distance[:, TILE - 1 :]
    bias = jnp.pad(by_distance.reshape(pairs, 2, TILE), ((0, 0), (0, 6), (0, 0)))
    router_wide = jnp.pad(router_weight, ((0, 0), (0, TILE - experts)))
    route_row = route.reshape(1, tokens)
    arrive_row = arrival[0]
    blocks = shape((experts, block_rows, width), bf16)
    block_space = pltpu.VMEM((experts, block_rows, width), bf16)
    block_sems = pltpu.SemaphoreType.DMA((2, experts - 1))
    any_space = pl.BlockSpec(memory_space=pl.ANY)

    slot_row, cot_sent, normed_own, normed_all, queries, keys, values, att, lse = pl.pallas_call(
        functools.partial(front_kernel, capacity),
        out_shape=[
            shape((1, tokens), jnp.int32),
            blocks,
            shape((tokens, width), bf16),
            shape((plen, width), bf16),
            shape((tokens, width), bf16),
            shape((keys_total, width), bf16),
            shape((keys_total, width), bf16),
            shape((width, tokens), bf16),
            shape((pairs, 8, tokens), f32),
        ],
        in_specs=[smem()] + [vmem()] * 9,
        out_specs=[vmem()] * 9,
        scratch_shapes=[
            pltpu.VMEM((ctx_count, PB, width), bf16),
            block_space,
            pltpu.VMEM((keys_total, tokens), f32),
            pltpu.VMEM((keys_total, tokens), bf16),
            pltpu.SemaphoreType.DMA((2, 2, ctx_count - 1, CHUNKS)),
            block_sems,
        ],
        compiler_params=remote_params(1),
        cost_estimate=cost(40 * keys_total * tokens * width, 20 * width * width),
        name="front",
    )(
        branch, bias, x, cot, attn_gain_row, route_row, arrive_row,
        query_weight, key_weight, value_weight,
    )
    cot_all = lax.all_gather(cot_sent, "dp", axis=0, tiled=False)

    members = 2 * lax.axis_size("expert") if ctx_count % 2 == 0 else experts
    group_rows = members * block_rows
    (
        rows_sent, router_part, hidden_grad, wo_part, att_grad, delta, moe_gain_part,
        result, hidden,
    ) = pl.pallas_call(
        functools.partial(expert_kernel, experts),
        out_shape=[
            blocks, shape((TILE, width), f32), shape((tokens, width), f32), shape((width // 16, 16, width), bf16),
            shape((tokens, width), bf16), shape((pairs, 8, tokens), f32), shape((1, width), f32),
            blocks, shape((tokens, width), f32),
        ],
        in_specs=[vmem()] * 8 + [any_space] * 2,
        out_specs=[vmem()] * 9,
        scratch_shapes=[
            pltpu.VMEM((tokens, width), bf16),
            block_space,
            pltpu.VMEM((width, hidden_units), bf16),
            pltpu.VMEM((hidden_units, width), bf16),
            pltpu.VMEM((group_rows, width), bf16),
            pltpu.VMEM((group_rows, width), bf16),
            pltpu.VMEM((group_rows, width), f32),
            pltpu.VMEM((group_rows, width), f32),
            block_space, block_space,
            pltpu.VMEM((tokens, width), bf16),
            pltpu.VMEM((width, tokens), bf16),
            block_sems, block_sems,
            pltpu.SemaphoreType.DMA((2,)),
        ],
        compiler_params=remote_params(2),
        cost_estimate=cost(8 * slots * width * hidden_units, 12 * width * hidden_units),
        name="expert",
    )(
        att, x, output_weight, moe_gain_row, router_wide, slot_row, cot, cot_sent,
        expert_in[0], expert_out[0],
    )
    att_grad, cot_all = lax.optimization_barrier((att_grad, cot_all))

    expert_count = lax.axis_size("expert")
    dp_sizes = [2, 2] if dp_count == 4 else [dp_count]
    sizes = [expert_count, *dp_sizes, ctx_count]
    plan = tail_plan(sizes, width)
    group, pieces, lengths = plan
    units = group * pieces

    stacked = 2 if ctx_count <= 4 else 1
    table_rows = heads * TILE // width
    small_rows = -(-(2 + experts + table_rows) // 8) * 8
    slice_width = hidden_units // dp_count
    weights, small, input_grad, in_grad, out_grad, layer_out, _ = pl.pallas_call(
        functools.partial(back_kernel, experts, plan),
        out_shape=[
            shape((units, 16, width), bf16), shape((small_rows, width), f32), shape((tokens, width), f32),
            shape((width, slice_width), f32), shape((slice_width, width), f32), shape((tokens, width), bf16),
            shape((dp_count - 1, experts, block_rows, width), bf16),
        ],
        in_specs=[
            smem(), vmem(), vmem(), any_space, any_space, vmem(), vmem(), vmem(), any_space, vmem(),
            vmem(), vmem(), vmem(), vmem(), any_space, vmem(), any_space, any_space, any_space,
            any_space, vmem(), any_space, any_space, any_space, any_space, any_space, vmem(),
        ],
        out_specs=[vmem()] * 6 + [any_space],
        scratch_shapes=[
            pltpu.VMEM((2, PB, width), bf16),
            pltpu.VMEM((2, PB, width), bf16),
            pltpu.VMEM((2, PB, width), bf16),
            pltpu.VMEM((stacked * PB, tokens), f32),
            pltpu.VMEM((stacked * PB, tokens), f32),
            pltpu.VMEM((stacked * PB, tokens), bf16),
            pltpu.VMEM((stacked * PB, tokens), bf16),
            pltpu.VMEM((width, tokens), f32),
            pltpu.VMEM((PB, width), bf16),
            pltpu.VMEM((PB, width), bf16),
            pltpu.VMEM((TILE, width), bf16),
            pltpu.VMEM((TILE, width), bf16),
            pltpu.VMEM((PB, TILE), bf16),
            pltpu.VMEM((heads, 8, TILE), f32),
            pltpu.VMEM((1, width), f32),
            pltpu.VMEM((tokens, width), f32),
            pltpu.VMEM((ctx_count - 1 if ctx_count <= 4 else 1, PB, width), bf16),
            pltpu.VMEM((ctx_count - 1, PB, width), bf16),
            pltpu.VMEM((units, 16, width), bf16),
            [pltpu.VMEM((pieces, length, 16, width), bf16) for length in lengths[:-1]],
            [
                pltpu.VMEM((pieces, size - 1, length, 16, width), bf16)
                for size, length in zip(sizes, lengths)
            ],
            pltpu.VMEM((small_rows, width), f32),
            [pltpu.VMEM((size - 1, small_rows, width), f32) for size in (expert_count, dp_count, ctx_count)],
            block_space,
            pltpu.VMEM((width, slice_width), bf16),
            pltpu.VMEM((slice_width, width), bf16),
            pltpu.VMEM((slots, width), bf16),
            pltpu.VMEM((slots, width), bf16),
            pltpu.VMEM((width, slots), bf16),
            pltpu.SemaphoreType.DMA((ctx_count + 2, 3)),
            pltpu.SemaphoreType.DMA((9 + 2 * dp_count,)),
            pltpu.SemaphoreType.DMA((2, 2 * pieces * sum(size - 1 for size in sizes))),
            pltpu.SemaphoreType.DMA((2, expert_count + dp_count + ctx_count - 3)),
            pltpu.SemaphoreType.DMA((2, ctx_count - 1)),
            block_sems,
            pltpu.SemaphoreType.DMA((2, dp_count - 1, experts)),
        ],
        compiler_params=remote_params(0),
        cost_estimate=cost(
            8 * dp_count * slots * width * slice_width + 80 * keys_total * tokens * width,
            60 * width * slice_width,
        ),
        name="back",
    )(
        branch, bias, queries, keys, values, att_grad, lse, delta, normed_all, normed_own,
        attn_gain_row, query_weight, key_weight, value_weight, wo_part, moe_gain_part, router_part, x,
        hidden_grad, hidden, slot_row, result,
        rows_sent, cot_all, expert_in[0], expert_out[0], router_wide,
    )

    matrix_units = width // 16
    steps = 8

    def part_rows(rows, columns=width):
        return pl.BlockSpec((rows // steps, columns), lambda i: (i, 0))

    weights = weights[: 4 * matrix_units].reshape(4, matrix_units, 16, width)
    *weights, in_grad, out_grad, input_grad, layer_out = pl.pallas_call(
        finish_kernel,
        grid=(steps,),
        out_shape=[shape((width, width), f32)] * 4
        + [
            shape((width, slice_width), f32), shape((slice_width, width), f32),
            shape((tokens, width), f32), shape((tokens, width), bf16),
        ],
        in_specs=[
            pl.BlockSpec((4, matrix_units // steps, 16, width), lambda i: (0, i, 0, 0)),
            part_rows(width, slice_width), part_rows(slice_width), part_rows(tokens), part_rows(tokens),
        ],
        out_specs=[part_rows(width)] * 4
        + [part_rows(width, slice_width), part_rows(slice_width), part_rows(tokens), part_rows(tokens)],
        compiler_params=params(),
        cost_estimate=cost(8 * width * width, 48 * width * width),
        name="finish",
    )(weights, in_grad, out_grad, input_grad, layer_out)
    router_grad = small[:experts].T
    hist_sum = small[2 + experts : 2 + experts + table_rows].reshape(heads, TILE)
    last = onehot[:, buckets - 1 :]
    spread = jnp.concatenate([onehot[:, : buckets - 1], last - 1.0], axis=1)
    table_grad = jnp.dot(spread.T, hist_sum.T, precision=lax.Precision.HIGHEST)
    return (
        layer_out[None],
        input_grad[None],
        small[experts],
        weights[3],
        weights[2],
        weights[1],
        weights[0],
        table_grad,
        small[experts + 1],
        router_grad,
        in_grad[None],
        out_grad[None],
    )


def solution(mesh):
    grouped = P(("dp", "expert"), "ctx", None)
    placed = (
        grouped, grouped, grouped, grouped, P(("dp", "expert"), "ctx"),
        P(), P(), P(), P(), P(), P(), P(), P(),
        P(("ctx", "expert"), None, None),
        P(("ctx", "expert"), None, None),
    )
    return jax.shard_map(
        body,
        mesh=mesh,
        in_specs=placed,
        out_specs=(
            grouped, grouped, P(), P(), P(), P(), P(), P(), P(), P(),
            P(("ctx", "expert"), None, "dp"),
            P(("ctx", "expert"), "dp", None),
        ),
        check_vma=False,
    )
```

profile of v0, /device:TPU:0, one launch (start us, length us, event | category | flops | bytes accessed | tf_op | source)
XLA Modules:
  0.0 284.8 jit_solution(3429688362764371953)
XLA Ops:
  7.2 0.0 copy-start
  7.2 0.0 all-gather.3.cloned.1.call-start
  7.3 0.6 copy-done
  7.9 0.1 convolution_bitcast_fusion
  8.0 0.2 slice_reduce_fusion
  8.2 0.1 broadcast_subtract_fusion
  8.3 1.3 reshape.107.gain_ref
  10.2 0.6 pad.8.bias_ref
  10.8 0.0 copy-start.2
  10.8 0.0 copy-start.3
  10.8 63.0 %front.1 = (s32[1,512]{1,0:T(1,128)}, bf16[8,72,768]{2,1,0:T(8,128)(2,1)}, bf16[512,768]{1,0:T(8,128)(2,1)}, bf16[1024,768]{1,0:T(8,128)(2,1)}, bf16[512,768]{1,...) custom-call(s32[1,1]{1,0:T(1,128)S(6)} %copy.30.branch_ref, ...), custom_call_target="tpu_custom_call" | custom-call | flops 22145925120 | bytes 11796480 | tf_op jit(solution)/shard_map/front/pallas_call | solution.py:1163
  73.9 0.0 all-gather.3.cloned.1.call-update
  73.9 0.0 copy-done.2
  73.9 0.2 copy.29
  74.1 0.0 copy-done.3
  74.1 0.6 reshape.109.gain_ref
  74.6 0.7 pad.9.router_ref
  75.4 50.3 %expert.1 = (bf16[8,72,768]{2,1,0:T(8,128)(2,1)}, f32[128,768]{1,0:T(8,128)}, f32[512,768]{1,0:T(8,128)}, bf16[48,16,768]{2,1,0:T(8,128)(2,1)}, bf16[512,768]{1,...) custom-call(bf16[768,512]{1,0:T(8,128)(2,1)} %get-tuple-element.49.a, ...), custom_call_target="tpu_custom_call" | custom-call | flops 10871635968 | bytes 28311552 | tf_op jit(solution)/shard_map/expert/pallas_call | solution.py:1200
  125.7 0.0 all-gather.3.cloned.1.call-done
  125.8 136.1 %back.1 = (bf16[192,16,768]{2,1,0:T(8,128)(2,1)}, f32[16,768]{1,0:T(8,128)}, f32[512,768]{1,0:T(8,128)}, f32[768,768]{1,0:T(8,128)}, f32[768,768]{1,0:T(8,128)},...) custom-call(s32[1,1]{1,0:T(1,128)S(6)} %copy.30.branch_ref, f32[6,8,128]{2,1,0:T(8,128)} %pad.8.bias_ref, ...), custom_call_target="tpu_custom_call" | custom-call | flops 55163486208 | bytes 35389440 | tf_op jit(solution)/shard_map/back/pallas_call | solution.py:1244
  261.9 0.7 slice.25
  262.6 1.3 slice_bitcast_fusion
  264.0 1.4 slice_reduce_fusion.1
  265.4 0.7 fusion
  266.2 0.0 copy-start.1
  266.2 11.6 %finish.1 = (f32[768,768]{1,0:T(8,128)}, f32[768,768]{1,0:T(8,128)}, f32[768,768]{1,0:T(8,128)}, f32[768,768]{1,0:T(8,128)}, f32[768,768]{1,0:T(8,128)}, /*index...) custom-call(bf16[4,48,16,768]{3,2,1,0:T(8,128)(2,1)} %bitcast.19, f32[768,768]{1,0:T(8,128)} %get-tuple-element.67.in_ref, ...), custom_call_target="tpu_custom_call" | custom-call | flops 4718592 | bytes 28311552 | tf_op jit(solution)/shard_map/finish/pallas_call | solution.py:1318
  277.7 0.0 copy-done.1
  (5 shorter events, 0.1 us)
Async XLA Ops:
  7.2 0.7 copy-start
  7.2 118.6 %all-gather.3.cloned.1.call-start = ((), (), s32[]{:S(2)}) async-start(), calls=%async_computation | async-start | bytes 4423680 | tf_op jit(solution)/shard_map/all_gather | solution.py:1193
  10.8 63.1 %copy-start.2 = (bf16[768,8]{0,1:T(8,128)(2,1)S(1)}, bf16[768,8]{0,1:T(8,128)(2,1)}, u32[]{:S(2)}) copy-start(bf16[768,8]{0,1:T(8,128)(2,1)} %param.27) | copy-start | bytes 36868
  10.8 63.3 %copy-start.3 = (bf16[768]{0:T(1024)(128)(2,1)S(1)}, bf16[768]{0:T(1024)(128)(2,1)}, u32[]{:S(2)}) copy-start(bf16[768]{0:T(1024)(128)(2,1)} %param.26) | copy-start | bytes 4612
  266.2 11.6 %copy-start.1 = (bf16[32,12]{0,1:T(8,128)(2,1)S(1)}, bf16[32,12]{0,1:T(8,128)(2,1)}, u32[]{:S(2)}) copy-start(bf16[32,12]{0,1:T(8,128)(2,1)} %param.25) | copy-start | bytes 2308
Sparse Core Ops, SparseCore 0:
  74.0 46.6 all-gather.2
where the time goes:
time: 290 us; the launch traced here: 285 us
  Pallas kernels  261 us (90%)
  between operations  15 us (5%)
  local copies, waits for them, and re-layouts  7.7 us (3%)
    pallas_call x1, Pallas kernels, body(): pl.pallas_call(functools.partial(back_kernel, experts, plan), out_shape=[...  136 us
    pallas_call x1, Pallas kernels, body(): pl.pallas_call(functools.partial(front_kernel, capacity), out_shape=[shap...  63 us
    pallas_call x1, Pallas kernels, body(): pl.pallas_call(functools.partial(expert_kernel, experts), out_shape=[bloc...  50.3 us
    pallas_call x1, Pallas kernels, body(): pl.pallas_call(finish_kernel, grid=(steps,), out_shape=[shape((width, wid...  11.6 us
  transfers between devices with their start and end apart: 1, of which 0 were waited for; matrix products, arithmetic and copies ran while one was open for 1% of the time, Pallas kernels for 18%

commit v1 on v0

--- a/solution.py
+++ b/solution.py
@@ -283,7 +283,28 @@
         normed_out[rows, :] = (x * inverse_rms(x) * gain).astype(bf16)
         project(block)
 
+    def down(row):
+        column = jnp.broadcast_to(row[...].astype(f32), (TILE, tokens)).T
+        return jnp.concatenate([column] * (tokens // TILE), axis=1)
+
+    same = down(route_row) == route_row[...].astype(f32)
+    earlier = down(arrive_row) < arrive_row[...].astype(f32)
+    rank = jnp.sum(jnp.where(same & earlier, 1.0, 0.0), axis=0, keepdims=True).astype(jnp.int32)
+    slot = jnp.where(rank < capacity, route_row[...] * block_rows + rank, count * block_rows)
+    slot_out[...] = slot
+
+    def lay_out(peer, _):
+        rows = dot_nn(place_rows(slot_out[...], peer, block_rows, tokens), cot_ref[...]).astype(bf16)
+        send_ref[peer] = rows
+        return 0
+
+    def lay_out_all():
+        lax.fori_loop(0, count, lay_out, 0)
+        cot_out[me] = send_ref[me]
+
     for step in range(ctx_count - 1):
+        if step == ctx_count - 2:
+            lay_out_all()
         for c in range(CHUNKS):
             for up in (True, False):
                 fits, block, copy = arrival(step, up, c)
@@ -298,26 +319,12 @@
             fits, block, copy = arrival(step, up, 0)
             pl.when(fits)(functools.partial(take, block))
 
-    def down(row):
-        column = jnp.broadcast_to(row[...].astype(f32), (TILE, tokens)).T
-        return jnp.concatenate([column] * (tokens // TILE), axis=1)
-
-    same = down(route_row) == route_row[...].astype(f32)
-    earlier = down(arrive_row) < arrive_row[...].astype(f32)
-    rank = jnp.sum(jnp.where(same & earlier, 1.0, 0.0), axis=0, keepdims=True).astype(jnp.int32)
-    slot = jnp.where(rank < capacity, route_row[...] * block_rows + rank, count * block_rows)
-    slot_out[...] = slot
-
-    def send_cot(ahead, _):
-        peer = lax.rem(me + ahead, count)
-        place = place_rows(slot_out[...], peer, block_rows, tokens)
-        send_ref[peer] = dot_nn(place, cot_ref[...]).astype(bf16)
-        block_copy(send_ref, cot_out, cot_sems, ahead).start()
-        return 0
-
     def send_cots():
+        def send_cot(ahead, _):
+            block_copy(send_ref, cot_out, cot_sems, ahead).start()
+            return 0
+
         lax.fori_loop(1, count, send_cot, 0)
-        cot_out[me] = dot_nn(place_rows(slot_out[...], me, block_rows, tokens), cot_ref[...]).astype(bf16)
 
     def window_column(i, _):
         cols = pl.ds(pl.multiple_of(i * 256, 256), 256)
@@ -429,9 +436,11 @@
         copy.start()
     greet_owners()
 
+    moe_ref[...] = att_ref[...].T
+
     def column(i, _):
         cols = pl.ds(pl.multiple_of(i * 256, 256), 256)
-        hidden_ref[:, cols] = x_ref[:, cols].astype(f32) + dot_tn(att_ref[...], wo_ref[:, cols])
+        hidden_ref[:, cols] = x_ref[:, cols].astype(f32) + dot_nn(moe_ref[...], wo_ref[:, cols])
         return 0
 
     lax.fori_loop(0, width // 256, column, 0)
@@ -754,7 +763,7 @@
     early = pieces > 1 and group <= rows_16
     begin = [blocks + j // 2 for j in range(pieces)]
     if early:
-        begin = [blocks - 1] + [blocks + (j - 1) // 2 for j in range(1, pieces)]
+        begin = [blocks - 1] + [blocks + (j - 1) // 3 for j in range(1, pieces)]
     pending = {}
 
     def advance(time):
@@ -1106,12 +1115,29 @@
     each_row_block(lambda copy: copy.wait_send())
 
 
-def finish_kernel(full_ref, in_ref, out_ref, input_ref, layer_ref, *results):
-    weights, rest = results[:4], results[4:]
+def finish_kernel(
+    experts, full_ref, in_ref, out_ref, input_ref, layer_ref, small_ref, spread_ref, *results,
+):
+    weights, rest, (attn_out, moe_out, router_out, table_out) = results[:4], results[4:8], results[8:]
     for n, weight in enumerate(weights):
         weight[...] = full_ref[n].astype(f32).reshape(weight.shape)
     for source, target in zip((in_ref, out_ref, input_ref, layer_ref), rest):
-        target[...] = source[...]
+        target[...] = source[...].astype(target.dtype)
+
+    @pl.when(pl.program_id(0) == 0)
+    def _():
+        router_out[...] = small_ref[:experts, :]
+        attn_out[...] = small_ref[experts : experts + 1, :]
+        moe_out[...] = small_ref[experts + 1 : experts + 2, :]
+        per_row = small_ref.shape[1] // TILE
+        hist = []
+        for head in range(table_out.shape[0]):
+            row, lane = 2 + experts + head // per_row, head % per_row * TILE
+            hist.append(small_ref[row : row + 1, lane : lane + TILE])
+        table_out[...] = jnp.dot(
+            jnp.concatenate(hist, axis=0), spread_ref[...],
+            preferred_element_type=f32, precision=lax.Precision.HIGHEST,
+        )
 
 
 def tail_plan(sizes, width):
@@ -1309,46 +1335,54 @@
     )
 
     matrix_units = width // 16
-    steps = 8
+    steps = 4
 
     def part_rows(rows, columns=width):
         return pl.BlockSpec((rows // steps, columns), lambda i: (i, 0))
 
     weights = weights[: 4 * matrix_units].reshape(4, matrix_units, 16, width)
-    *weights, in_grad, out_grad, input_grad, layer_out = pl.pallas_call(
-        finish_kernel,
+    last = onehot[:, buckets - 1 :]
+    spread = jnp.concatenate([onehot[:, : buckets - 1], last - 1.0], axis=1)
+
+    def same(rows, columns):
+        return pl.BlockSpec((rows, columns), lambda i: (0, 0))
+
+    (
+        *weights, in_grad, out_grad, input_grad, layer_out, attn_gain_grad, moe_gain_grad, router_grad, table_grad,
+    ) = pl.pallas_call(
+        functools.partial(finish_kernel, experts),
         grid=(steps,),
         out_shape=[shape((width, width), f32)] * 4
         + [
             shape((width, slice_width), f32), shape((slice_width, width), f32),
             shape((tokens, width), f32), shape((tokens, width), bf16),
+            shape((1, width), f32), shape((1, width), f32), shape((experts, width), f32), shape((heads, buckets), f32),
         ],
         in_specs=[
-            pl.BlockSpec((4, matrix_units // steps, 16, width), lambda i: (0, i, 0, 0)),
+            pl.BlockSpec(
+                (4, matrix_units // steps, 16, width), lambda i: (0, i, 0, 0)
+            ),
             part_rows(width, slice_width), part_rows(slice_width), part_rows(tokens), part_rows(tokens),
+            same(small_rows, width), same(TILE, buckets),
         ],
         out_specs=[part_rows(width)] * 4
-        + [part_rows(width, slice_width), part_rows(slice_width), part_rows(tokens), part_rows(tokens)],
+        + [part_rows(width, slice_width), part_rows(slice_width), part_rows(tokens), part_rows(tokens)]
+        + [same(1, width), same(1, width), same(experts, width), same(heads, buckets)],
         compiler_params=params(),
         cost_estimate=cost(8 * width * width, 48 * width * width),
         name="finish",
-    )(weights, in_grad, out_grad, input_grad, layer_out)
-    router_grad = small[:experts].T
-    hist_sum = small[2 + experts : 2 + experts + table_rows].reshape(heads, TILE)
-    last = onehot[:, buckets - 1 :]
-    spread = jnp.concatenate([onehot[:, : buckets - 1], last - 1.0], axis=1)
-    table_grad = jnp.dot(spread.T, hist_sum.T, precision=lax.Precision.HIGHEST)
+    )(weights, in_grad, out_grad, input_grad, layer_out, small, spread)
     return (
         layer_out[None],
         input_grad[None],
-        small[experts],
+        attn_gain_grad.reshape(width),
         weights[3],
         weights[2],
         weights[1],
         weights[0],
-        table_grad,
-        small[experts + 1],
-        router_grad,
+        table_grad.T,
+        moe_gain_grad.reshape(width),
+        router_grad.T,
         in_grad[None],
         out_grad[None],
     )

time: 290 us -> 292 us (level)
    pallas_call x1, Pallas kernels: 136 us -> 141 us  [body(): pl.pallas_call(functools.partial(back_kernel, experts, plan), out_shape=[...]
where the time goes in v1:
time: 292 us; the launch traced here: 286 us
  Pallas kernels  263 us (90%)
  between operations  15 us (5%)
  local copies, waits for them, and re-layouts  4.89 us (2%)
    pallas_call x1, Pallas kernels, body(): pl.pallas_call(functools.partial(back_kernel, experts, plan), out_shape=[...  141 us
    pallas_call x1, Pallas kernels, body(): pl.pallas_call(functools.partial(front_kernel, capacity), out_shape=[shap...  60.7 us
    pallas_call x1, Pallas kernels, body(): pl.pallas_call(functools.partial(expert_kernel, experts), out_shape=[bloc...  50.3 us
    pallas_call x1, Pallas kernels, body(): pl.pallas_call(functools.partial(finish_kernel, experts), grid=(steps,),...  11 us
  transfers between devices with their start and end apart: 1, of which 0 were waited for; matrix products, arithmetic and copies ran while one was open for 1% of the time, Pallas kernels for 18%

profile of v1, /device:TPU:0, one launch (start us, length us, event | category | flops | bytes accessed | tf_op | source)
XLA Modules:
  0.0 286.1 jit_solution(5539311943525948798)
XLA Ops:
  7.2 0.0 copy-start
  7.2 0.0 all-gather.3.cloned.1.call-start
  7.3 0.6 copy-done
  7.9 0.1 convolution_bitcast_fusion
  8.0 0.2 slice_reduce_fusion
  8.2 0.1 broadcast_subtract_fusion
  8.3 1.3 reshape.110.gain_ref
  10.2 0.6 pad.8.bias_ref
  10.8 0.0 copy-start.2
  10.8 0.0 copy-start.3
  10.8 60.7 %front.1 = (s32[1,512]{1,0:T(1,128)}, bf16[8,72,768]{2,1,0:T(8,128)(2,1)}, bf16[512,768]{1,0:T(8,128)(2,1)}, bf16[1024,768]{1,0:T(8,128)(2,1)}, bf16[512,768]{1,...) custom-call(s32[1,1]{1,0:T(1,128)S(6)} %copy.31.branch_ref, ...), custom_call_target="tpu_custom_call" | custom-call | flops 22145925120 | bytes 11796480 | tf_op jit(solution)/shard_map/front/pallas_call | solution.py:1189
  71.6 0.0 all-gather.3.cloned.1.call-update
  71.6 0.0 copy-done.2
  71.6 0.2 copy.29
  71.8 0.0 copy-done.3
  71.8 0.6 reshape.112.gain_ref
  72.4 0.7 copy.30.spread_ref
  73.1 0.7 pad.9.router_ref
  73.8 50.3 %expert.1 = (bf16[8,72,768]{2,1,0:T(8,128)(2,1)}, f32[128,768]{1,0:T(8,128)}, f32[512,768]{1,0:T(8,128)}, bf16[48,16,768]{2,1,0:T(8,128)(2,1)}, bf16[512,768]{1,...) custom-call(bf16[768,512]{1,0:T(8,128)(2,1)} %get-tuple-element.53.a, ...), custom_call_target="tpu_custom_call" | custom-call | flops 10871635968 | bytes 28311552 | tf_op jit(solution)/shard_map/expert/pallas_call | solution.py:1226
  124.1 0.0 all-gather.3.cloned.1.call-done
  124.1 141.3 %back.1 = (bf16[192,16,768]{2,1,0:T(8,128)(2,1)}, f32[16,768]{1,0:T(8,128)}, f32[512,768]{1,0:T(8,128)}, f32[768,768]{1,0:T(8,128)}, f32[768,768]{1,0:T(8,128)},...) custom-call(s32[1,1]{1,0:T(1,128)S(6)} %copy.31.branch_ref, f32[6,8,128]{2,1,0:T(8,128)} %pad.8.bias_ref, ...), custom_call_target="tpu_custom_call" | custom-call | flops 55163486208 | bytes 35389440 | tf_op jit(solution)/shard_map/back/pallas_call | solution.py:1270
  265.5 0.0 copy-start.1
  265.5 11.0 %finish.1 = (f32[768,768]{1,0:T(8,128)}, f32[768,768]{1,0:T(8,128)}, f32[768,768]{1,0:T(8,128)}, f32[768,768]{1,0:T(8,128)}, f32[768,768]{1,0:T(8,128)}, /*index...) custom-call(bf16[4,48,16,768]{3,2,1,0:T(8,128)(2,1)} %bitcast.18, ...), custom_call_target="tpu_custom_call" | custom-call | flops 4718592 | bytes 28311552 | tf_op jit(solution)/shard_map/finish/pallas_call | solution.py:1352
  276.5 1.3 reduce.1
  277.8 1.3 reduce.2
  279.0 0.0 copy-done.1
  (5 shorter events, 0.1 us)
Async XLA Ops:
  7.2 0.7 copy-start
  7.2 116.9 %all-gather.3.cloned.1.call-start = ((), (), s32[]{:S(2)}) async-start(), calls=%async_computation | async-start | bytes 4423680 | tf_op jit(solution)/shard_map/all_gather | solution.py:1219
  10.8 60.8 %copy-start.2 = (bf16[768,8]{0,1:T(8,128)(2,1)S(1)}, bf16[768,8]{0,1:T(8,128)(2,1)}, u32[]{:S(2)}) copy-start(bf16[768,8]{0,1:T(8,128)(2,1)} %param.27) | copy-start | bytes 36868
  10.8 61.0 %copy-start.3 = (bf16[768]{0:T(1024)(128)(2,1)S(1)}, bf16[768]{0:T(1024)(128)(2,1)}, u32[]{:S(2)}) copy-start(bf16[768]{0:T(1024)(128)(2,1)} %param.26) | copy-start | bytes 4612
  265.5 13.6 %copy-start.1 = (bf16[32,12]{0,1:T(8,128)(2,1)S(1)}, bf16[32,12]{0,1:T(8,128)(2,1)}, u32[]{:S(2)}) copy-start(bf16[32,12]{0,1:T(8,128)(2,1)} %param.25) | copy-start | bytes 2308
Sparse Core Ops, SparseCore 0:
  71.7 46.5 all-gather.2

commit v2 on v1

--- a/solution.py
+++ b/solution.py
@@ -763,7 +763,7 @@
     early = pieces > 1 and group <= rows_16
     begin = [blocks + j // 2 for j in range(pieces)]
     if early:
-        begin = [blocks - 1] + [blocks + (j - 1) // 3 for j in range(1, pieces)]
+        begin = [blocks - 2] + [blocks - 1 + (j - 1) // 2 for j in range(1, pieces)]
     pending = {}
 
     def advance(time):
@@ -979,6 +979,8 @@
             shared_copies.append(
                 push(shared_send.at[n % shared_slots], shared_recv.at[n], shared_sems, n, lines.peer(remote))
             )
+        if early and i == blocks - 2:
+            advance(i)
     started.extend(shared_copies[-shared_slots:])
 
     def ready(j):

time: 292 us -> 285 us (0.976)
  the two profiles are of different devices: /device:TPU:0 before, /device:TPU:25 now
where the time goes in v2:
time: 285 us; the launch traced here: 281 us
  Pallas kernels  258 us (91%)
  between operations  15 us (5%)
  local copies, waits for them, and re-layouts  4.89 us (2%)
    pallas_call x1, Pallas kernels, body(): pl.pallas_call(functools.partial(back_kernel, experts, plan), out_shape=[...  126 us
    pallas_call x1, Pallas kernels, body(): pl.pallas_call(functools.partial(expert_kernel, experts), out_shape=[bloc...  63.3 us
    pallas_call x1, Pallas kernels, body(): pl.pallas_call(functools.partial(front_kernel, capacity), out_shape=[shap...  57.6 us
    pallas_call x1, Pallas kernels, body(): pl.pallas_call(functools.partial(finish_kernel, experts), grid=(steps,),...  11 us
  transfers between devices with their start and end apart: 1, of which 0 were waited for; matrix products, arithmetic and copies ran while one was open for 1% of the time, Pallas kernels for 23%

profile of v2, /device:TPU:25, one launch (start us, length us, event | category | flops | bytes accessed | tf_op | source)
XLA Modules:
  0.0 281.1 jit_solution(10576598241578463628)
XLA Ops:
  7.2 0.0 copy-start
  7.2 0.0 all-gather.3.cloned.1.call-start
  7.3 0.6 copy-done
  7.9 0.1 convolution_bitcast_fusion
  8.0 0.2 slice_reduce_fusion
  8.2 0.1 broadcast_subtract_fusion
  8.3 1.3 reshape.110.gain_ref
  10.2 0.6 pad.8.bias_ref
  10.8 0.0 copy-start.2
  10.8 0.0 copy-start.3
  10.8 57.6 %front.1 = (s32[1,512]{1,0:T(1,128)}, bf16[8,72,768]{2,1,0:T(8,128)(2,1)}, bf16[512,768]{1,0:T(8,128)(2,1)}, bf16[1024,768]{1,0:T(8,128)(2,1)}, bf16[512,768]{1,...) custom-call(s32[1,1]{1,0:T(1,128)S(6)} %copy.31.branch_ref, ...), custom_call_target="tpu_custom_call" | custom-call | flops 22145925120 | bytes 11796480 | tf_op jit(solution)/shard_map/front/pallas_call | solution.py:1191
  68.4 0.0 all-gather.3.cloned.1.call-update
  68.4 0.0 copy-done.2
  68.4 0.2 copy.29
  68.6 0.0 copy-done.3
  68.6 0.6 reshape.112.gain_ref
  69.2 0.7 copy.30.spread_ref
  69.9 0.7 pad.9.router_ref
  70.7 63.3 %expert.1 = (bf16[8,72,768]{2,1,0:T(8,128)(2,1)}, f32[128,768]{1,0:T(8,128)}, f32[512,768]{1,0:T(8,128)}, bf16[48,16,768]{2,1,0:T(8,128)(2,1)}, bf16[512,768]{1,...) custom-call(bf16[768,512]{1,0:T(8,128)(2,1)} %get-tuple-element.53.a, ...), custom_call_target="tpu_custom_call" | custom-call | flops 10871635968 | bytes 28311552 | tf_op jit(solution)/shard_map/expert/pallas_call | solution.py:1228
  133.9 0.0 all-gather.3.cloned.1.call-done
  134.0 126.5 %back.1 = (bf16[192,16,768]{2,1,0:T(8,128)(2,1)}, f32[16,768]{1,0:T(8,128)}, f32[512,768]{1,0:T(8,128)}, f32[768,768]{1,0:T(8,128)}, f32[768,768]{1,0:T(8,128)},...) custom-call(s32[1,1]{1,0:T(1,128)S(6)} %copy.31.branch_ref, f32[6,8,128]{2,1,0:T(8,128)} %pad.8.bias_ref, ...), custom_call_target="tpu_custom_call" | custom-call | flops 55163486208 | bytes 35389440 | tf_op jit(solution)/shard_map/back/pallas_call | solution.py:1272
  260.5 0.0 copy-start.1
  260.5 11.0 %finish.1 = (f32[768,768]{1,0:T(8,128)}, f32[768,768]{1,0:T(8,128)}, f32[768,768]{1,0:T(8,128)}, f32[768,768]{1,0:T(8,128)}, f32[768,768]{1,0:T(8,128)}, /*index...) custom-call(bf16[4,48,16,768]{3,2,1,0:T(8,128)(2,1)} %bitcast.18, ...), custom_call_target="tpu_custom_call" | custom-call | flops 4718592 | bytes 28311552 | tf_op jit(solution)/shard_map/finish/pallas_call | solution.py:1354
  271.5 1.3 reduce.1
  272.8 1.3 reduce.2
  274.1 0.0 copy-done.1
  (5 shorter events, 0.1 us)
Async XLA Ops:
  7.2 0.7 copy-start
  7.2 126.8 %all-gather.3.cloned.1.call-start = ((), (), s32[]{:S(2)}) async-start(), calls=%async_computation | async-start | bytes 4423680 | tf_op jit(solution)/shard_map/all_gather | solution.py:1221
  10.8 57.6 %copy-start.2 = (bf16[768,8]{0,1:T(8,128)(2,1)S(1)}, bf16[768,8]{0,1:T(8,128)(2,1)}, u32[]{:S(2)}) copy-start(bf16[768,8]{0,1:T(8,128)(2,1)} %param.27) | copy-start | bytes 36868
  10.8 57.8 %copy-start.3 = (bf16[768]{0:T(1024)(128)(2,1)S(1)}, bf16[768]{0:T(1024)(128)(2,1)}, u32[]{:S(2)}) copy-start(bf16[768]{0:T(1024)(128)(2,1)} %param.26) | copy-start | bytes 4612
  260.5 13.6 %copy-start.1 = (bf16[32,12]{0,1:T(8,128)(2,1)S(1)}, bf16[32,12]{0,1:T(8,128)(2,1)}, u32[]{:S(2)}) copy-start(bf16[32,12]{0,1:T(8,128)(2,1)} %param.25) | copy-start | bytes 2308
Sparse Core Ops, SparseCore 0:
  68.6 47.9 all-gather.2
